TPU v7x, 128 devices: a whole 4x4x4 slice. The times are simulated.
128 devices in a mesh: row: 8 (over y_lo, x), col: 16 (over z, y_hi, core).
Axes of the slice: x: 4, y: 4 (y_hi: 2, y_lo: 2; y = y_hi * 2 + y_lo), z: 4, core: 2. Of those that a mesh axis runs over, the one named last changes fastest.
Arguments:
- amplitudes: float32 [16, 3, 1024, 1024], P('row', None, 'col'), may hold values from -6 to 6
- dressing: float32 [1024, 1024], replicated, may hold values from -0.1875 to 0.1875
- integrals: float32 [1024, 3, 16384], P('row', None, 'col'), may hold values from -0.109375 to 0.109375
- occupied_energy: float32 [128], replicated, may hold values from -2 to -0.3
- virtual_energy: float32 [1024], replicated, may hold values from 0.2 to 3
- occupied_rows: int32 [16], P('row'), may hold values from 0 to 127
- virtual_rows: int32 [1024], replicated, may hold values from 0 to 1023
- occupied_columns: int32 [16], P('col'), may hold values from 0 to 127
- virtual_columns: int32 [1024], replicated, may hold values from 0 to 1023
Outputs:
- residual: float32 [16384, 16384], P('row', 'col')
All inputs are finite; a program needn't handle non-finite values.
Results may differ from a plain program's by a relative error of at most 0.00007.
Values sent between devices are 32-bit elements; how exact they have to be, the bound alone decides.
A program may use at most 128 MiB of HBM per device.

v0:
```python
import functools

import jax
import jax.numpy as jnp
from jax import lax
from jax.experimental import pallas as pl
from jax.experimental.pallas import tpu as pltpu
from jax.sharding import PartitionSpec as P

MESH = pl.DeviceIdType.MESH
BF16, F32 = jnp.bfloat16, jnp.float32
WIDTH = 512
PIECE = 64

SEND, WAIT, DRESSING, DRESS, ENERGY, SPLIT, FULL, HALF = range(8)
XP, XM, ZP, ZM, Y = range(5)
INT, AMP = range(2)
PLAN = (
    (SEND, XP, INT, 0, 0, 0, 0), (SEND, XP, INT, 0, 0, 0, 1), (SEND, XM, INT, 0, 0, 0, 1),
    (SEND, XM, INT, 0, 0, 0, 0), (SEND, Y, INT, 0, 0, 0, 0), (SEND, Y, INT, 0, 0, 0, 1),
    (SEND, Y, INT, 1, 0, 0, 0), (DRESSING,), (DRESS, 0), (SEND, XP, INT, 1, 0, 0, 0),
    (SEND, XM, INT, 1, 0, 0, 1), (SEND, ZP, AMP, 0, 0, 0, 0), (SEND, ZP, AMP, 0, 0, 0, 1),
    (SEND, ZM, AMP, 0, 0, 0, 1), (SEND, ZM, AMP, 0, 0, 0, 0), (SEND, Y, AMP, 0, 0, 0, 0), (DRESS, 1),
    (WAIT, INT, 0, 3, 0, 0), (WAIT, INT, 0, 1, 0, 1), (WAIT, INT, 0, 0, 1, 0), (DRESS, 2), (ENERGY,),
    (SEND, XP, INT, 0, 3, 0, 0), (SEND, XM, INT, 0, 1, 0, 1), (SEND, Y, AMP, 0, 0, 0, 1),
    (SEND, ZP, AMP, 1, 0, 0, 0), (SEND, ZM, AMP, 1, 0, 0, 1), (WAIT, INT, 0, 3, 0, 1),
    (WAIT, INT, 0, 1, 0, 0), (WAIT, INT, 0, 0, 1, 1), (WAIT, AMP, 0, 3, 0, 0), (WAIT, AMP, 0, 1, 0, 1),
    (SEND, XP, INT, 0, 0, 1, 0), (SEND, XM, INT, 0, 0, 1, 1), (SEND, Y, AMP, 1, 0, 0, 0),
    (SEND, ZP, AMP, 0, 3, 0, 0), (SEND, ZM, AMP, 0, 1, 0, 1), (WAIT, INT, 1, 3, 0, 0),
    (WAIT, INT, 1, 1, 0, 1), (WAIT, INT, 1, 0, 1, 0), (WAIT, AMP, 0, 3, 0, 1), (WAIT, AMP, 0, 1, 0, 0),
    (SEND, XP, INT, 0, 0, 1, 1), (SEND, XM, INT, 0, 0, 1, 0), (SEND, Y, INT, 1, 0, 0, 1),
    (SEND, ZP, AMP, 1, 0, 0, 1), (SEND, ZM, AMP, 1, 0, 0, 0), (WAIT, INT, 0, 2, 0, 0),
    (WAIT, INT, 0, 2, 0, 1), (WAIT, AMP, 0, 0, 1, 0), (SPLIT, 0, 0), (WAIT, AMP, 1, 3, 0, 0),
    (WAIT, AMP, 1, 1, 0, 1), (HALF, 0, 0, 0, 0), (HALF, 0, 1, 0, 0), (HALF, 0, 3, 0, 0),
    (SEND, XP, INT, 1, 0, 0, 1), (SEND, XM, INT, 1, 0, 0, 0), (SEND, Y, AMP, 1, 0, 0, 1),
    (SEND, ZP, AMP, 0, 0, 1, 0), (SEND, ZM, AMP, 0, 0, 1, 0), (WAIT, INT, 0, 3, 1, 0),
    (WAIT, INT, 0, 1, 1, 1), (WAIT, AMP, 0, 0, 1, 1), (WAIT, AMP, 0, 2, 0, 0), (WAIT, AMP, 0, 2, 0, 1),
    (HALF, 0, 0, 1, 0), (HALF, 0, 2, 0, 0), (SEND, XP, INT, 0, 3, 1, 0), (SEND, XM, INT, 0, 1, 1, 1),
    (SEND, Y, INT, 2, 0, 0, 0), (SEND, ZP, AMP, 0, 0, 1, 1), (SEND, ZM, AMP, 0, 0, 1, 1),
    (WAIT, INT, 0, 3, 1, 1), (WAIT, INT, 0, 1, 1, 0), (WAIT, AMP, 1, 0, 1, 0), (WAIT, AMP, 1, 3, 0, 1),
    (WAIT, AMP, 1, 1, 0, 0), (SEND, XP, INT, 1, 3, 0, 0), (SEND, XM, INT, 1, 1, 0, 1),
    (SEND, Y, AMP, 2, 0, 0, 0), (SEND, ZP, AMP, 1, 3, 0, 0), (SEND, ZM, AMP, 1, 1, 0, 1),
    (WAIT, INT, 1, 3, 0, 1), (WAIT, INT, 1, 1, 0, 0), (WAIT, INT, 1, 0, 1, 1), (WAIT, AMP, 0, 3, 1, 0),
    (WAIT, AMP, 0, 1, 1, 0), (SEND, XP, INT, 1, 0, 1, 0), (SEND, XM, INT, 1, 0, 1, 1),
    (SEND, Y, INT, 2, 0, 0, 1), (SEND, ZP, AMP, 0, 3, 1, 0), (SEND, ZM, AMP, 1, 0, 1, 0),
    (WAIT, INT, 0, 2, 1, 0), (WAIT, INT, 0, 2, 1, 1), (WAIT, AMP, 1, 0, 1, 1), (SPLIT, 0, 1),
    (WAIT, AMP, 0, 3, 1, 1), (WAIT, AMP, 0, 1, 1, 1), (HALF, 0, 0, 0, 1), (HALF, 0, 0, 1, 1), (FULL, 0, 1, 1),
    (SEND, XP, INT, 1, 0, 1, 1), (SEND, XM, INT, 1, 0, 1, 0), (SEND, Y, AMP, 2, 0, 0, 1), (FULL, 0, 3, 1),
    (WAIT, INT, 1, 2, 0, 0), (WAIT, INT, 1, 2, 0, 1), (WAIT, INT, 2, 0, 1, 0), (WAIT, AMP, 1, 2, 0, 0),
    (WAIT, AMP, 1, 2, 0, 1), (SEND, ZP, AMP, 1, 0, 1, 0), (SEND, ZM, AMP, 0, 1, 1, 1), (HALF, 0, 1, 0, 1),
    (HALF, 0, 2, 0, 1), (HALF, 0, 3, 0, 1), (SEND, XP, INT, 2, 0, 0, 0), (SEND, XM, INT, 2, 0, 0, 1),
    (SEND, Y, INT, 1, 2, 0, 0), (SPLIT, 1, 0), (WAIT, INT, 1, 3, 1, 0), (WAIT, INT, 1, 1, 1, 1),
    (WAIT, AMP, 2, 0, 1, 0), (SEND, ZP, AMP, 1, 0, 1, 1), (SEND, ZM, AMP, 1, 0, 1, 1), (HALF, 1, 0, 0, 0),
    (WAIT, AMP, 0, 2, 1, 0), (WAIT, AMP, 1, 1, 1, 0), (HALF, 1, 0, 1, 0), (HALF, 1, 1, 0, 0),
    (HALF, 1, 2, 0, 0), (SEND, XP, INT, 2, 0, 0, 1), (SEND, XM, INT, 2, 0, 0, 0), (SEND, Y, INT, 1, 2, 0, 1),
    (HALF, 1, 3, 0, 0), (WAIT, INT, 1, 3, 1, 1), (WAIT, INT, 1, 1, 1, 0), (WAIT, INT, 2, 0, 1, 1),
    (SEND, ZP, AMP, 2, 0, 0, 0), (SEND, ZM, AMP, 2, 0, 0, 1), (WAIT, AMP, 1, 3, 1, 0),
    (WAIT, AMP, 0, 2, 1, 1), (FULL, 0, 2, 1), (SEND, XP, INT, 2, 0, 1, 0), (SEND, XM, INT, 2, 0, 1, 1),
    (SEND, Y, AMP, 1, 2, 0, 0), (SEND, ZP, AMP, 2, 0, 0, 1), (SEND, ZM, AMP, 2, 0, 0, 0),
    (WAIT, INT, 2, 3, 0, 0), (WAIT, INT, 2, 1, 0, 1), (WAIT, AMP, 2, 0, 1, 1), (WAIT, AMP, 1, 3, 1, 1),
    (WAIT, AMP, 1, 1, 1, 1), (HALF, 1, 3, 1, 0), (HALF, 1, 1, 1, 0), (SEND, XP, INT, 2, 3, 0, 0),
    (SEND, XM, INT, 2, 1, 0, 1), (SEND, Y, AMP, 1, 2, 0, 1), (SEND, ZP, AMP, 2, 0, 1, 0),
    (SEND, ZM, AMP, 2, 0, 1, 1), (WAIT, INT, 2, 3, 0, 1), (WAIT, INT, 2, 1, 0, 0), (WAIT, INT, 1, 2, 1, 0),
    (WAIT, AMP, 2, 3, 0, 0), (WAIT, AMP, 2, 1, 0, 1), (SEND, XP, INT, 2, 0, 1, 1),
    (SEND, XM, INT, 2, 0, 1, 0), (SEND, ZP, AMP, 2, 3, 0, 0), (SEND, ZM, AMP, 2, 1, 0, 1),
    (WAIT, INT, 2, 3, 1, 0), (WAIT, INT, 2, 1, 1, 1), (WAIT, INT, 1, 2, 1, 1), (SPLIT, 1, 1),
    (WAIT, AMP, 2, 3, 0, 1), (WAIT, AMP, 2, 1, 0, 0), (HALF, 1, 0, 0, 1), (HALF, 1, 0, 1, 1),
    (HALF, 1, 1, 0, 1), (HALF, 1, 1, 1, 1), (SEND, XP, INT, 2, 3, 1, 0), (SEND, XM, INT, 2, 1, 1, 1),
    (SEND, ZP, AMP, 2, 0, 1, 1), (SEND, ZM, AMP, 2, 0, 1, 0), (HALF, 1, 2, 0, 1), (WAIT, INT, 2, 2, 0, 0),
    (WAIT, INT, 2, 2, 0, 1), (WAIT, AMP, 1, 2, 1, 0), (WAIT, AMP, 2, 3, 1, 0), (WAIT, AMP, 2, 1, 1, 1),
    (HALF, 1, 3, 0, 1), (HALF, 1, 3, 1, 1), (SPLIT, 2, 0), (HALF, 2, 0, 0, 0), (SEND, ZP, AMP, 2, 3, 1, 0),
    (SEND, ZM, AMP, 2, 1, 1, 1), (HALF, 2, 0, 1, 0), (WAIT, INT, 2, 3, 1, 1), (WAIT, INT, 2, 1, 1, 0),
    (WAIT, AMP, 1, 2, 1, 1), (WAIT, AMP, 2, 2, 0, 0), (WAIT, AMP, 2, 2, 0, 1), (HALF, 2, 1, 0, 0),
    (HALF, 2, 3, 0, 0), (FULL, 1, 2, 1), (HALF, 2, 2, 0, 0), (WAIT, INT, 2, 2, 1, 0), (WAIT, INT, 2, 2, 1, 1),
    (SPLIT, 2, 1), (WAIT, AMP, 2, 3, 1, 1), (WAIT, AMP, 2, 1, 1, 0), (HALF, 2, 0, 0, 1), (HALF, 2, 0, 1, 1),
    (FULL, 2, 1, 1), (FULL, 2, 3, 1), (WAIT, AMP, 2, 2, 1, 0), (WAIT, AMP, 2, 2, 1, 1), (HALF, 2, 1, 0, 1),
    (HALF, 2, 2, 0, 1), (FULL, 2, 2, 1), (HALF, 2, 3, 0, 1),
)


def parts(values):
    high = values.astype(BF16)
    return high, (values - high.astype(F32)).astype(BF16)


def dot(a, b):
    return jnp.dot(a, b, preferred_element_type=F32)


def dot3(a, b_high, b_low):
    a_high, a_low = parts(a)
    return dot(a_high, b_high) + dot(a_high, b_low) + dot(a_low, b_high)


def column(row):
    tiles = [
        jnp.transpose(jnp.broadcast_to(row[:, at : at + 128], (128, 128)))
        for at in range(0, row.shape[1], 128)
    ]
    return jnp.concatenate(tiles, axis=0)


def kernel(
    amp,
    dressing,
    w_in,
    occupied_energy,
    virtual_energy,
    occupied_rows,
    virtual_rows,
    occupied_columns,
    virtual_columns,
    C,
    A,
    W,
    SH,
    SL,
    EA,
    EB,
    EI,
    send_sem,
    recv_w,
    recv_a,
    local_sem,
    out_sem,
):
    row, col = lax.axis_index("row"), lax.axis_index("col")
    x, ylo = row % 4, row // 4
    z, yhi, core = col // 4, (col // 2) % 2, col % 2

    def source_row(dx, dy):
        return ((ylo + dy) % 2) * 4 + (x + dx) % 4

    def source_col(dz, dy, dcore):
        return ((z + dz) % 4) * 4 + ((yhi + dy) % 2) * 2 + (core + dcore) % 2

    xp, xm, yl = (source_row(1, 0), col), (source_row(3, 0), col), (source_row(0, 1), col)
    zp, zm = (row, source_col(1, 0, 0)), (row, source_col(3, 0, 0))
    yh, sib = (row, source_col(0, 1, 0)), (row, source_col(0, 0, 1))
    neighbours = (xp, xm, yl, zp, zm, yh, sib)

    def rows_w(r, h):
        return pl.ds(pl.multiple_of(r * 128 + h * PIECE, PIECE), PIECE)

    def rows_a(s):
        return pl.ds(pl.multiple_of(s * PIECE, PIECE), PIECE)

    counts = [0, 0, 0]

    def copy_w(k, r, h, target, own=False):
        return pltpu.make_async_remote_copy(
            src_ref=w_in.at[k, pl.ds(h * PIECE, PIECE)] if own else W.at[k, rows_w(r, h)],
            dst_ref=W.at[k, rows_w(r, h)],
            send_sem=send_sem.at[k],
            recv_sem=recv_w.at[k, 2 * r + h],
            device_id=target,
            device_id_type=MESH,
        )

    def copy_a(k, i, s, target):
        return pltpu.make_async_remote_copy(
            src_ref=A.at[k, i, rows_a(s)],
            dst_ref=A.at[k, i, rows_a(s)],
            send_sem=send_sem.at[k],
            recv_sem=recv_a.at[k, i, s],
            device_id=target,
            device_id_type=MESH,
        )

    def send_w(k, r, h, *targets, own=False):
        for target in targets:
            copy_w(k, r, h, target, own).start()
            counts[k] += 1

    def send_a(k, i, s, *targets):
        for target in targets:
            copy_a(k, i, s, target).start()
            counts[k] += 1

    def wait_w(k, r, h):
        copy_w(k, r, h, yl).wait_recv()

    def wait_a(k, i, s):
        copy_a(k, i, s, sib).wait_recv()

    own_w, own_a = source_row(0, 0), source_col(0, 0, 0)

    def split(source, slot, first, count):
        def one(step, _):
            rows = pl.ds(pl.multiple_of(first + step * 64, 64), 64)
            high, low = parts(source[rows])
            SH[slot, rows] = high
            SL[slot, rows] = low
            return 0

        lax.fori_loop(0, count // 64, one, 0)

    def update(k, dz, dy, depth_at=0, depth=1024):
        group = ((z + dz) % 4) * 2 + (yhi + dy) % 2
        rows = pl.ds(pl.multiple_of(group * 128, 128), 128)
        if depth == 1024:
            inner = slice(None)
        else:
            inner = pl.ds(pl.multiple_of(depth_at, depth), depth)
        before = parts_done[dz, dy]
        parts_done[dz, dy] = before + depth // 512
        last = parts_done[dz, dy] == 6

        def one(step, _):
            columns = pl.ds(pl.multiple_of(step * WIDTH, WIDTH), WIDTH)
            a = A[k, :, rows, inner].reshape(256, depth)
            value = dot3(a, SH[k, inner, columns], SL[k, inner, columns])
            value = value.reshape(2, 128, WIDTH)
            if before == 0:
                C[:, rows, columns] = value
            elif not last:
                C[:, rows, columns] += value
            else:
                sums = jnp.concatenate([EA[rows]] * (WIDTH // 128), axis=1) + EB[0:1, columns]
                level_j = EI[2:3, 0:1]
                for i in (0, 1):
                    denominator = (sums - EI[i : i + 1, 0:1]) - level_j
                    C[i, rows, columns] = (C[i, rows, columns] + value[i]) / denominator
            return 0

        lax.fori_loop(0, 1024 // WIDTH, one, 0)

    chunk = 256
    loads = [
        pltpu.make_async_copy(
            dressing.at[pl.ds(at, chunk)], C.at[0, pl.ds(at, chunk)], local_sem.at[at // chunk]
        )
        for at in range(0, 1024, chunk)
    ]
    amp_loads = [
        pltpu.make_async_copy(amp.at[:, k], A.at[k, :, rows_a(own_a)], local_sem.at[4 + k])
        for k in range(3)
    ]
    w_load = pltpu.make_async_copy(
        w_in, W.at[:, pl.ds(pl.multiple_of(own_w * 128, 128), 128)], local_sem.at[7]
    )
    for load in (*loads, *amp_loads, w_load):
        load.start()
    barrier = pltpu.get_barrier_semaphore()
    for target in neighbours:
        pl.semaphore_signal(barrier, inc=1, device_id=target, device_id_type=MESH)
    pl.semaphore_wait(barrier, len(neighbours))

    def split_dressing():
        for number, load in enumerate(loads):
            load.wait()
            split(C.at[0], 2, number * chunk, chunk)

    def dress(k):
        amp_loads[k].wait()
        dressed = dot3(A[k, :, rows_a(own_a)].reshape(128, 1024), SH[2], SL[2])
        A[k, :, rows_a(own_a)] = dressed.reshape(2, PIECE, 1024)


    def energies():
        table = virtual_energy[...]
        lanes = lax.broadcasted_iota(jnp.int32, (128, 1024), 1)
        for at in range(0, 1024, 128):
            index = column(virtual_rows[:, at : at + 128])
            index = jnp.concatenate([index] * 8, axis=1)
            found = jnp.sum(jnp.where(index == lanes, table, 0.0), axis=1, keepdims=True)
            EA[at : at + 128] = jnp.broadcast_to(found, (128, 128))
            index = column(virtual_columns[:, at : at + 128])
            index = jnp.concatenate([index] * 8, axis=1)
            found = jnp.sum(jnp.where(index == lanes, table, 0.0), axis=1, keepdims=True)
            found = jnp.transpose(jnp.broadcast_to(found, (128, 128)))
            EB[:, at : at + 128] = found[:8]
        places = lax.broadcasted_iota(jnp.int32, (1, 128), 1)
        levels = (occupied_rows[0], occupied_rows[1], occupied_columns[0])
        for number, place in enumerate(levels):
            level = jnp.sum(
                jnp.where(places == place, occupied_energy[...], 0.0), axis=1, keepdims=True
            )
            EI[number : number + 1] = jnp.broadcast_to(level, (1, 128))

    links = {XP: xp, XM: xm, ZP: zp, ZM: zm}
    parts_done = {(d, dy): 0 for d in range(4) for dy in (0, 1)}
    seen, w_loaded = set(), [False]
    for step, *rest in PLAN:
        if step == SEND:
            link, array, k, d, dy, h = rest
            if array == INT:
                send_w(k, source_row(d, dy), h, links.get(link, yl), own=(d, dy) == (0, 0))
            else:
                send_a(k, h, source_col(d, dy, 0), links.get(link, yh))
        elif step == WAIT:
            array, k, d, dy, h = rest
            if array == INT:
                wait_w(k, source_row(d, dy), h)
            else:
                wait_a(k, h, source_col(d, dy, 0))
                send_a(k, h, source_col(d, dy, 0), sib)
        elif step == DRESSING:
            split_dressing()
        elif step == DRESS:
            (k,) = rest
            dress(k)
            for i in (0, 1):
                send_a(k, i, own_a, sib)
        elif step == ENERGY:
            energies()
        elif step == SPLIT:
            k, dy = rest
            if not w_loaded[0]:
                w_load.wait()
                w_loaded[0] = True
            split(W.at[k], k, ((ylo + dy) % 2) * 512, 512)
        else:
            k, dz, dy, *half = rest
            if (k, dz, dy) not in seen:
                seen.add((k, dz, dy))
                for i in (0, 1):
                    wait_a(k, i, source_col(dz, dy, 1))
            if half:
                update(k, dz, dy, ((ylo + half[0]) % 2) * 512, 512)
            else:
                update(k, dz, dy)

    for k in range(3):
        share = A.at[0:2, :, pl.ds(0, counts[k] * PIECE // 4)]
        pltpu.make_async_remote_copy(
            src_ref=share,
            dst_ref=share,
            send_sem=send_sem.at[k],
            recv_sem=recv_a.at[0, 0, 0],
            device_id=sib,
            device_id_type=MESH,
        ).wait_send()


def on_device(
    amplitudes,
    dressing,
    integrals,
    occupied_energy,
    virtual_energy,
    occupied_rows,
    virtual_rows,
    occupied_columns,
    virtual_columns,
):
    anywhere = pl.BlockSpec(memory_space=pl.ANY)
    vmem = pl.BlockSpec(memory_space=pltpu.VMEM)
    smem = pl.BlockSpec(memory_space=pltpu.SMEM)
    residual = pl.pallas_call(
        kernel,
        out_shape=pltpu.VMEM((2, 1024, 1024), F32),
        in_specs=[anywhere, anywhere, anywhere, vmem, vmem, smem, vmem, smem, vmem],
        out_specs=vmem,
        scratch_shapes=[
            pltpu.VMEM((3, 2, 1024, 1024), F32),
            pltpu.VMEM((3, 1024, 1024), F32),
            pltpu.VMEM((3, 1024, 1024), BF16),
            pltpu.VMEM((3, 1024, 1024), BF16),
            pltpu.VMEM((1024, 128), F32),
            pltpu.VMEM((8, 1024), F32),
            pltpu.VMEM((8, 128), F32),
            pltpu.SemaphoreType.DMA((3,)),
            pltpu.SemaphoreType.DMA((3, 16)),
            pltpu.SemaphoreType.DMA((3, 2, 16)),
            pltpu.SemaphoreType.DMA((8,)),
            pltpu.SemaphoreType.DMA((8,)),
        ],
        compiler_params=pltpu.CompilerParams(
            collective_id=0, has_side_effects=True, vmem_limit_bytes=55 * 2**20
        ),
        cost_estimate=pl.CostEstimate(
            flops=42_000_000_000, bytes_accessed=20_000_000, transcendentals=0
        ),
    )(
        amplitudes,
        dressing,
        jnp.transpose(integrals, (1, 0, 2)),
        occupied_energy.reshape(1, -1),
        virtual_energy.reshape(1, -1),
        occupied_rows,
        virtual_rows.reshape(1, -1),
        occupied_columns,
        virtual_columns.reshape(1, -1),
    )
    return residual.reshape(2048, 1024)


def solution(mesh):
    return jax.shard_map(
        on_device,
        mesh=mesh,
        in_specs=(
            P("row", None, "col", None),
            P(),
            P("row", None, "col"),
            P(),
            P(),
            P("row"),
            P(),
            P("col"),
            P(),
        ),
        out_specs=P("row", "col"),
        check_vma=False,
    )
```

profile of v0, /device:TPU:1, one launch (start us, length us, event | category | flops | bytes accessed | tf_op | source)
XLA Modules:
  0.0 123.7 jit_solution(18231731868811754003)
XLA Ops:
  0.7 119.6 %shard_map.91 = f32[2,1024,1024]{2,1,0:T(8,128)S(1)} custom-call(f32[2,3,64,1024]{3,2,1,0:T(8,128)} %amp.1, f32[1024,1024]{1,0:T(8,128)} %dressing.1, f32[3,128,1024]{2,1,0:T(8,128)} %bitcast.7, f32[1,128]{1,0:T(1,128)} %bitcast.11, f32[1,1024]{1,0:T(1,128)} %bitcast.8, s32[2]{0:T(128)} %occupied_rows.1, s32[1,1024]{1,0:T(1,128)} %bitcast.9, ...), custom_call_target="tpu_custom_call" | custom-call | flops 41999998976 | bytes 20000000 | tf_op jit(solution)/shard_map/pallas_call | solution.py:350
  120.3 3.4 %copy.11 = f32[2048,1024]{1,0:T(8,128)} copy(f32[2048,1024]{1,0:T(8,128)S(1)} %bitcast.6) | data formatting | bytes 16777216
where the time goes:
time: 124 us
  Pallas kernels  120 us (97%)
  local copies, waits for them, and re-layouts  3.4 us (3%)
    pallas_call x1, Pallas kernels, on_device(): pl.pallas_call(kernel, out_shape=pltpu.VMEM((2, 1024, 1024), F32), in_spe...  120 us
    unnamed x1, local copies, waits for them, and re-layouts  3.4 us

commit v1 on v0

--- a/solution.py
+++ b/solution.py
@@ -9,7 +9,7 @@
 
 MESH = pl.DeviceIdType.MESH
 BF16, F32 = jnp.bfloat16, jnp.float32
-WIDTH = 512
+WIDTHS = (512, 512, 1024)
 PIECE = 64
 
 SEND, WAIT, DRESSING, DRESS, ENERGY, SPLIT, FULL, HALF = range(8)
@@ -206,24 +206,29 @@
         parts_done[dz, dy] = before + depth // 512
         last = parts_done[dz, dy] == 6
 
+        width = WIDTHS[k]
+
         def one(step, _):
-            columns = pl.ds(pl.multiple_of(step * WIDTH, WIDTH), WIDTH)
+            columns = slice(None) if width == 1024 else pl.ds(pl.multiple_of(step * width, width), width)
             a = A[k, :, rows, inner].reshape(256, depth)
             value = dot3(a, SH[k, inner, columns], SL[k, inner, columns])
-            value = value.reshape(2, 128, WIDTH)
+            value = value.reshape(2, 128, width)
             if before == 0:
                 C[:, rows, columns] = value
             elif not last:
                 C[:, rows, columns] += value
             else:
-                sums = jnp.concatenate([EA[rows]] * (WIDTH // 128), axis=1) + EB[0:1, columns]
+                sums = jnp.concatenate([EA[rows]] * (width // 128), axis=1) + EB[0:1, columns]
                 level_j = EI[2:3, 0:1]
                 for i in (0, 1):
                     denominator = (sums - EI[i : i + 1, 0:1]) - level_j
                     C[i, rows, columns] = (C[i, rows, columns] + value[i]) / denominator
             return 0
 
-        lax.fori_loop(0, 1024 // WIDTH, one, 0)
+        if width == 1024:
+            one(0, 0)
+        else:
+            lax.fori_loop(0, 1024 // width, one, 0)
 
     chunk = 256
     loads = [

time: 124 us -> 122 us (0.984)
  Pallas kernels: 120 us -> 118 us
    pallas_call x1, Pallas kernels: 120 us -> 118 us  [on_device(): pl.pallas_call(kernel, out_shape=pltpu.VMEM((2, 1024, 1024), F32), in_spe...]
where the time goes in v1:
time: 122 us
  Pallas kernels  118 us (97%)
  local copies, waits for them, and re-layouts  3.4 us (3%)
    pallas_call x1, Pallas kernels, on_device(): pl.pallas_call(kernel, out_shape=pltpu.VMEM((2, 1024, 1024), F32), in_spe...  118 us
    unnamed x1, local copies, waits for them, and re-layouts  3.4 us

profile of v1, /device:TPU:1, one launch (start us, length us, event | category | flops | bytes accessed | tf_op | source)
XLA Modules:
  0.0 121.9 jit_solution(9845767404414677559)
XLA Ops:
  0.7 117.8 %shard_map.91 = f32[2,1024,1024]{2,1,0:T(8,128)S(1)} custom-call(f32[2,3,64,1024]{3,2,1,0:T(8,128)} %amp.1, f32[1024,1024]{1,0:T(8,128)} %dressing.1, f32[3,128,1024]{2,1,0:T(8,128)} %bitcast.7, f32[1,128]{1,0:T(1,128)} %bitcast.11, f32[1,1024]{1,0:T(1,128)} %bitcast.8, s32[2]{0:T(128)} %occupied_rows.1, s32[1,1024]{1,0:T(1,128)} %bitcast.9, ...), custom_call_target="tpu_custom_call" | custom-call | flops 41999998976 | bytes 20000000 | tf_op jit(solution)/shard_map/pallas_call | solution.py:355
  118.5 3.4 %copy.11 = f32[2048,1024]{1,0:T(8,128)} copy(f32[2048,1024]{1,0:T(8,128)S(1)} %bitcast.6) | data formatting | bytes 16777216
